TPU v7x, 256 devices: a whole 4x4x8 slice. The times are simulated.
256 devices in a mesh: gs: 64 (over z, y, core), view: 4 (over x).
Axes of the slice: x: 4, y: 4, z: 8, core: 2. Of those that a mesh axis runs over, the one named last changes fastest.
Arguments:
- gaussians: float32 [59, 262144], P(None, 'gs'), may hold values from -6 to 1.5, as said below
- send_index: int32 [4, 4096, 128], P('view', 'gs'), may hold values from 0 to 4095
- tile_list: int32 [4, 512, 256], P('view', 'gs'), may hold values from 0 to 8191
- tile_length: int32 [4, 512], P('view', 'gs'), may hold values from 32 to 256, as said below
- camera: float32 [4, 5], P('view'), may hold values from -3.140625 to 3.140625
- exposure: float32 [4, 5], P('view'), may hold values from 0.25 to 4
- target: float32 [4, 15, 1024, 128], P('view', None, 'gs'), may hold values from 0 to 1
Outputs:
- param_grad: float32 [59, 262144], P(None, 'gs')
- radiance: float32 [4, 3, 1024, 128], P('view', None, 'gs')
Inputs may be any that keep to these rules, and one draw needn't show every extreme that they name: `gaussians`: Rows: position within [-1, 1], log scales within [-1, 0.5], quaternion w within [0.5, 1.5] and x, y, z within [-0.5, 0.5], opacity logit within [-6, -2], degree-0 harmonic coefficients within [-1, 1], the others within [-0.2, 0.2]. `tile_length`: every renderer's first tile uses all 256 entries.
All inputs are finite; a program needn't handle non-finite values.
Results may differ from a plain program's by a relative error of at most 0.0003.
Values sent between devices are 32-bit elements; how exact they have to be, the bound alone decides.
A program may use at most 128 MiB of HBM per device.

v0:
```python
import functools

import jax
import jax.numpy as jnp
import numpy as np
from jax import lax
from jax.experimental import pallas as pl
from jax.experimental.pallas import tpu as pltpu
from jax.sharding import PartitionSpec as P

MESH = pl.DeviceIdType.MESH
F32, BF16, I32 = jnp.float32, jnp.bfloat16, jnp.int32

FOCAL = 16.0
DILATE = 0.3
SH_C0 = 0.28209479177387814
SH_C1 = 0.4886025119029199
SH_C2 = [
    1.0925484305920792,
    -1.0925484305920792,
    0.31539156525252005,
    -1.0925484305920792,
    0.5462742152960396,
]
SH_C3 = [
    -0.5900435899266435,
    2.890611442640554,
    -0.4570457994644658,
    0.3731763325901154,
    -0.4570457994644658,
    1.445305721320277,
    -0.5900435899266435,
]
WINDOW_RAW = np.exp(-((np.arange(11) - 5.0) ** 2) / 4.5)
WINDOW = [float(v) for v in WINDOW_RAW / WINDOW_RAW.sum()]
FLOOR_MEAN = 0.0001
FLOOR_VAR = 0.0009

FEAT = 59
SPLAT = 9
HIGH = 32
TILES = 8
LIST = 256
ROWS = 16
COLS = 128
CHANNELS = 15
FIRST = 11
MAPS = 26


def product3(left, right):
    return [[sum((left[i][k] * right[k][j] for k in range(3))) for j in range(3)] for i in range(3)]


def camera_rotation(camera):
    yaw_cos, yaw_sin = (jnp.cos(camera[0]), jnp.sin(camera[0]))
    pitch_cos, pitch_sin = (jnp.cos(camera[1]), jnp.sin(camera[1]))
    roll_cos, roll_sin = (jnp.cos(camera[2]), jnp.sin(camera[2]))
    about_z = [[yaw_cos, -yaw_sin, 0.0], [yaw_sin, yaw_cos, 0.0], [0.0, 0.0, 1.0]]
    about_y = [[pitch_cos, 0.0, pitch_sin], [0.0, 1.0, 0.0], [-pitch_sin, 0.0, pitch_cos]]
    about_x = [[1.0, 0.0, 0.0], [0.0, roll_cos, -roll_sin], [0.0, roll_sin, roll_cos]]
    return product3(product3(about_z, about_y), about_x)


def quaternion_matrix(q0, q1, q2, q3):
    scale = 1.0 / jnp.sqrt(q0 * q0 + q1 * q1 + q2 * q2 + q3 * q3)
    w, x, y, z = (q0 * scale, q1 * scale, q2 * scale, q3 * scale)
    return [
        [1 - 2 * (y * y + z * z), 2 * (x * y - w * z), 2 * (x * z + w * y)],
        [2 * (x * y + w * z), 1 - 2 * (x * x + z * z), 2 * (y * z - w * x)],
        [2 * (x * z - w * y), 2 * (y * z + w * x), 1 - 2 * (x * x + y * y)],
    ]


def harmonics(x, y, z):
    xx, yy, zz = (x * x, y * y, z * z)
    return [
        SH_C0 + 0.0 * x,
        -SH_C1 * y,
        SH_C1 * z,
        -SH_C1 * x,
        SH_C2[0] * x * y,
        SH_C2[1] * y * z,
        SH_C2[2] * (2 * zz - xx - yy),
        SH_C2[3] * x * z,
        SH_C2[4] * (xx - yy),
        SH_C3[0] * y * (3 * xx - yy),
        SH_C3[1] * x * y * z,
        SH_C3[2] * y * (4 * zz - xx - yy),
        SH_C3[3] * z * (2 * zz - 3 * xx - 3 * yy),
        SH_C3[4] * x * (4 * zz - xx - yy),
        SH_C3[5] * z * (xx - yy),
        SH_C3[6] * x * (xx - 3 * yy),
    ]


def project(params, camera, rotation):
    translation = [0.15 * camera[3], 0.15 * camera[4], 6.0]
    position = [params[i] for i in range(3)]
    viewed = [
        sum((rotation[i][j] * position[j] for j in range(3))) + translation[i] for i in range(3)
    ]
    inverse_z = 1.0 / viewed[2]
    row_x = [
        FOCAL * inverse_z * (rotation[0][k] - viewed[0] * inverse_z * rotation[2][k])
        for k in range(3)
    ]
    row_y = [
        FOCAL * inverse_z * (rotation[1][k] - viewed[1] * inverse_z * rotation[2][k])
        for k in range(3)
    ]
    orient = quaternion_matrix(params[6], params[7], params[8], params[9])
    stretch = [jnp.exp(params[3 + k]) for k in range(3)]
    image_x = [sum((row_x[i] * orient[i][k] for i in range(3))) * stretch[k] for k in range(3)]
    image_y = [sum((row_y[i] * orient[i][k] for i in range(3))) * stretch[k] for k in range(3)]
    cov_xx = sum((e * e for e in image_x)) + DILATE
    cov_yy = sum((e * e for e in image_y)) + DILATE
    cov_xy = sum((image_x[k] * image_y[k] for k in range(3)))
    share = 1.0 / (cov_xx * cov_yy - cov_xy * cov_xy)
    opacity = 1.0 / (1.0 + jnp.exp(-params[10]))
    toward = [
        position[k] + sum((rotation[i][k] * translation[i] for i in range(3))) for k in range(3)
    ]
    closeness = 1.0 / jnp.sqrt(sum((e * e for e in toward)))
    harmonic = harmonics(*[e * closeness for e in toward])
    colour = [
        jnp.exp(sum((harmonic[l] * params[11 + 3 * l + c] for l in range(16)))) for c in range(3)
    ]
    return [
        FOCAL * viewed[0] * inverse_z,
        FOCAL * viewed[1] * inverse_z,
        cov_yy * share,
        -cov_xy * share,
        cov_xx * share,
        opacity,
    ] + colour


def iota(shape, axis):
    return lax.broadcasted_iota(I32, shape, axis)


def lane_gather(values, index):
    return jnp.take_along_axis(values, index, axis=1, mode="promise_in_bounds")


def parts(values):
    top = values.astype(BF16)
    return top, (values - top.astype(F32)).astype(BF16)


def dot(left, right):
    return jnp.dot(left, right, preferred_element_type=F32)


def dot_nt(left, right):
    return lax.dot_general(left, right, (((1,), (1,)), ((), ())), preferred_element_type=F32)


def spread_rows(gauss_ref, wide_ref):
    def one(h, carry):
        lanes = pl.ds(pl.multiple_of(h * COLS, COLS), COLS)
        for first in range(0, FEAT, 8):
            count = min(8, FEAT - first)
            wide_ref[pl.ds(first * HIGH + h, count, stride=HIGH), :] = gauss_ref[first : first + count, lanes]
        return carry

    lax.fori_loop(0, HIGH, one, 0)


def window_columns():
    column = iota((1, COLS), 1)
    taps = []
    for i in range(11):
        source = column + (i - 5)
        taps.append(jnp.where((source >= 0) & (source < COLS), WINDOW[i], 0.0))
    return taps


def along_columns(values, taps):
    total = values * taps[5]
    for i in range(11):
        if i != 5:
            total = total + taps[i] * pltpu.roll(values, (5 - i) % COLS, axis=1)
    return total


def along_rows(ref, row):
    def at(i):
        return ref[pl.ds(pl.multiple_of((row + i) * 16, 16), 16), :]

    total = WINDOW[5] * at(0)
    for i in range(1, 6):
        total = total + WINDOW[5 + i] * (at(i) + at(-i))
    return total


def step_kernel(
    n,
    nv,
    gauss_ref,
    send_ref,
    list_ref,
    len_ref,
    cam_ref,
    expo_ref,
    target_ref,
    gall_ref,
    rad_ref,
    wide_ref,
    table_ref,
    pick_ref,
    out_ref,
    recv_ref,
    splat_ref,
    cover_ref,
    weight_ref,
    top_ref,
    low_ref,
    pair_ref,
    deriv_ref,
    tile_rad_ref,
    strips_ref,
    edge_ref,
    t_ref,
    tt_ref,
    p_ref,
    pp_ref,
    pt_ref,
    mt_ref,
    btt_ref,
    gm_ref,
    gpp_ref,
    gpt_ref,
    gimg_ref,
    gtile_ref,
    sgrad_ref,
    slot_one_ref,
    slot_mask_ref,
    own_one_ref,
    own_mask_ref,
    slot_left_ref,
    slot_sum_ref,
    back_ref,
    ret_ref,
    own_left_ref,
    own_sum_ref,
    gown_ref,
    f_send,
    f_recv,
    b_send,
    b_recv,
    t_send,
    t_recv,
    h_send,
    h_recv,
    v_send,
    v_recv,
):
    me = lax.axis_index("gs")
    mv = lax.axis_index("view")
    after = lax.rem(me + 1, n)
    before = lax.rem(me + n - 1, n)
    group = min(8, n)
    groups = n // group
    halves = slot_mask_ref.shape[0]

    barrier = pltpu.get_barrier_semaphore()

    def greet(i, carry):
        pl.semaphore_signal(
            barrier, inc=1, device_id={"gs": lax.rem(me + i, n)}, device_id_type=MESH
        )
        return carry

    lax.fori_loop(1, n, greet, 0)
    for i in range(1, nv):
        pl.semaphore_signal(
            barrier, inc=1, device_id={"view": lax.rem(mv + i, nv)}, device_id_type=MESH
        )

    spread_rows(gauss_ref, wide_ref)
    camera = [jnp.full((8, COLS), cam_ref[0, i], F32) for i in range(5)]
    rotation = camera_rotation(camera)

    def project_rows(i, carry):
        rows = [
            wide_ref[pl.ds(pl.multiple_of(f * HIGH + i * 8, 8), 8), :] for f in range(FEAT)
        ]
        for f, value in enumerate(project(rows, camera, rotation)):
            table_ref[pl.ds(pl.multiple_of(f * HIGH + i * 8, 8), 8), :] = value
        return carry

    lax.fori_loop(0, HIGH // 8, project_rows, 0)
    for i in range(5):
        gown_ref[SPLAT * HIGH + i : SPLAT * HIGH + i + 1, :] = camera[i][0:1]
    gown_ref[SPLAT * HIGH + 5 : SPLAT * HIGH + 8, :] = jnp.zeros((3, COLS), F32)

    pl.semaphore_wait(barrier, n - 1 + nv - 1)

    def target_copy(peer, side):
        return pltpu.make_async_remote_copy(
            src_ref=target_ref.at[0],
            dst_ref=edge_ref.at[side],
            send_sem=t_send.at[side],
            recv_sem=t_recv.at[side],
            device_id={"gs": peer},
            device_id_type=MESH,
        )

    def strip_copy(peer, side):
        return pltpu.make_async_remote_copy(
            src_ref=strips_ref.at[1],
            dst_ref=strips_ref.at[2 * side],
            send_sem=h_send.at[side],
            recv_sem=h_recv.at[side],
            device_id={"gs": peer},
            device_id_type=MESH,
        )

    @pl.when(me < n - 1)
    def _():
        target_copy(after, 0).start()

    @pl.when(me > 0)
    def _():
        target_copy(before, 1).start()

    def forward_copy(peer, slot):
        return pltpu.make_async_remote_copy(
            src_ref=out_ref.at[peer],
            dst_ref=recv_ref.at[slot],
            send_sem=f_send.at[peer],
            recv_sem=f_recv.at[slot],
            device_id={"gs": peer},
            device_id_type=MESH,
        )

    def back_copy(peer, slot):
        return pltpu.make_async_remote_copy(
            src_ref=back_ref.at[peer],
            dst_ref=ret_ref.at[slot],
            send_sem=b_send.at[peer],
            recv_sem=b_recv.at[slot],
            device_id={"gs": peer},
            device_id_type=MESH,
        )

    my_group = me // group

    def gather_group(step, carry):
        block = lax.rem(my_group + step, groups)
        index = send_ref[0, pl.ds(pl.multiple_of(block * group, group), group), :]
        high = index >> 7
        low = index & 127

        def one(h, totals):
            chosen = high == h
            new = []
            for f in range(SPLAT):
                row = jnp.broadcast_to(table_ref[pl.ds(f * HIGH + h, 1), :], (group, COLS))
                new.append(jnp.where(chosen, lane_gather(row, low), totals[f]))
            return tuple(new)

        totals = lax.fori_loop(
            0, HIGH, one, tuple(jnp.zeros((group, COLS), F32) for _ in range(SPLAT)), unroll=4
        )
        for f in range(SPLAT):
            pick_ref[f * group : (f + 1) * group, :] = totals[f]
        for i in range(group):
            peer = block * group + i
            out_ref[peer] = pick_ref[pl.ds(i, SPLAT, stride=group), :]
        for i in range(group):
            peer = block * group + lax.rem(me + i, group)

            @pl.when(peer != me)
            def _():
                forward_copy(peer, me).start()

        return carry

    lax.fori_loop(0, groups, gather_group, 0)
    recv_ref[me] = out_ref[me]

    def own_factors(r, carry):
        index = send_ref[0, pl.ds(r, 1), :]
        lanes = pl.ds(pl.multiple_of(r * COLS, COLS), COLS)
        own_one_ref[:, lanes] = jnp.where(iota((256, COLS), 0) == (index & 255), 1.0, 0.0).astype(BF16)
        own_mask_ref[:, lanes] = jnp.where(iota((16, COLS), 0) == (index >> 8), 1.0, 0.0).astype(BF16)
        return carry

    lax.fori_loop(0, n, own_factors, 0)

    def slot_factors(j, carry):
        index = list_ref[0, pl.ds(j, 1), :]
        lanes = pl.ds(pl.multiple_of(j * LIST, LIST), LIST)
        slot_one_ref[:, lanes] = jnp.where(iota((256, LIST), 0) == (index & 255), 1.0, 0.0).astype(BF16)
        slot_mask_ref[:, lanes] = jnp.where(iota((halves, LIST), 0) == (index >> 8), 1.0, 0.0).astype(
            BF16
        )
        return carry

    lax.fori_loop(0, TILES, slot_factors, 0)

    @pl.when(me == 0)
    def _():
        edge_ref[0] = jnp.zeros((CHANNELS, ROWS, COLS), F32)
        strips_ref[0] = jnp.zeros((3, ROWS, COLS), F32)

    @pl.when(me == n - 1)
    def _():
        edge_ref[1] = jnp.zeros((CHANNELS, ROWS, COLS), F32)
        strips_ref[2] = jnp.zeros((3, ROWS, COLS), F32)

    @pl.when(me > 0)
    def _():
        target_copy(before, 0).wait_recv()

    @pl.when(me < n - 1)
    def _():
        target_copy(after, 1).wait_recv()

    for strip in range(3):
        for ch in range(16):
            if ch == CHANNELS:
                value = jnp.zeros((ROWS, COLS), F32)
            elif strip == 1:
                value = target_ref[0, ch]
            else:
                value = edge_ref[strip // 2, ch]
            t_ref[pl.ds(strip * 256 + ch, ROWS, stride=16), :] = value

    taps = window_columns()

    def square_target(row, carry):
        rows = pl.ds(pl.multiple_of(row * 16, 16), 16)
        tt_ref[rows, :] = t_ref[rows, :] * t_ref[rows, :]
        return carry

    lax.fori_loop(FIRST - 5, FIRST + MAPS + 5, square_target, 0)

    def target_maps(i, carry):
        rows = pl.ds(pl.multiple_of(i * 16, 16), 16)
        mt_ref[rows, :] = along_columns(along_rows(t_ref, FIRST + i), taps)
        btt_ref[rows, :] = along_columns(along_rows(tt_ref, FIRST + i), taps)
        return carry

    lax.fori_loop(0, MAPS, target_maps, 0)

    owner = [list_ref[0, :, 128 * h : 128 * h + 128] >> 7 for h in range(2)]
    place = [list_ref[0, :, 128 * h : 128 * h + 128] & 127 for h in range(2)]

    def take_group(step, totals):
        block = lax.rem(my_group + groups - step, groups)
        for i in range(group):
            sender = block * group + i

            @pl.when(sender != me)
            def _():
                forward_copy(sender, sender).wait_recv()

        for i in range(group):
            sender = block * group + i
            chosen = [owner[h] == sender for h in range(2)]
            new = []
            for f in range(SPLAT):
                row = jnp.broadcast_to(recv_ref[sender, f : f + 1, :], (TILES, COLS))
                for h in range(2):
                    new.append(
                        jnp.where(chosen[h], lane_gather(row, place[h]), totals[2 * f + h])
                    )
            totals = tuple(new)
        return totals

    totals = lax.fori_loop(
        0, groups, take_group, tuple(jnp.zeros((TILES, COLS), F32) for _ in range(2 * SPLAT))
    )
    tile_row = iota((TILES, COLS), 0)
    length = jnp.zeros((TILES, COLS), I32)
    for j in range(TILES):
        length = jnp.where(tile_row == j, len_ref[0, j], length)
    for f in range(SPLAT):
        for h in range(2):
            splat_ref[f * TILES : (f + 1) * TILES, 128 * h : 128 * h + 128] = totals[2 * f + h]
    for h in range(2):
        active = (iota((TILES, COLS), 1) + 128 * h) < length
        splat_ref[SPLAT * TILES : (SPLAT + 1) * TILES, 128 * h : 128 * h + 128] = jnp.where(
            active, totals[2 * 5 + h], 0.0
        )

    def splat_row(f, j):
        return splat_ref[pl.ds(f * TILES + j, 1), :]

    column_x = iota((ROWS, LIST), 0).astype(F32) + (0.5 - 8.0)
    first_of = iota((LIST, LIST), 0)
    then_of = iota((LIST, LIST), 1)
    earlier = jnp.where(first_of < then_of, 1.0, 0.0).astype(BF16)
    earlier = jnp.concatenate([earlier, earlier], axis=0)
    later = jnp.where(first_of > then_of, 1.0, 0.0).astype(BF16)
    later = jnp.concatenate([later, later], axis=0)

    def pixel_rows(j, y):
        return pl.ds(pl.multiple_of(j * 256 + y * 16, 16), 16)

    def composite(j, carry):
        ox, oy, a, b, c = [splat_row(f, j) for f in range(5)]
        opacity = splat_row(SPLAT, j)
        dx = column_x - ox
        square_part = (-0.5 * a) * dx * dx
        cross_part = (-b) * dx
        for y in range(16):
            dy = (y + 0.5 - 8.0) - oy
            power = square_part + dy * cross_part + (-0.5 * c) * dy * dy
            cover = opacity * jnp.exp(power)
            cover_ref[pixel_rows(j, y), :] = cover
            top, low = parts(jnp.log(1.0 - cover))
            pair_ref[y * 16 : y * 16 + 16, 0:LIST] = top
            pair_ref[y * 16 : y * 16 + 16, LIST : 2 * LIST] = low
        deriv_ref[...] = dot(pair_ref[...], earlier)
        for y in range(16):
            rows = pixel_rows(j, y)
            cover = cover_ref[rows, :]
            weight = cover * jnp.exp(deriv_ref[y * 16 : y * 16 + 16, :])
            cover_ref[rows, :] = cover / (1.0 - cover)
            weight_ref[rows, :] = weight
            top, low = parts(weight)
            top_ref[rows, :] = top
            low_ref[rows, :] = low
        tile_rows = pl.ds(pl.multiple_of(j * 256, 256), 256)
        colours = jnp.concatenate([splat_row(6 + c, j) for c in range(3)], axis=0)
        colour_top = colours.astype(BF16).astype(F32)
        packed = jnp.concatenate(
            [colour_top, colours - colour_top, jnp.zeros((10, LIST), F32)], axis=0
        ).astype(BF16)
        seen = dot_nt(packed, top_ref[tile_rows, :]) + dot_nt(packed, low_ref[tile_rows, :])
        for c in range(3):
            tile_rad_ref[pl.ds(c * TILES + j, 1), :] = seen[c : c + 1] + seen[c + 3 : c + 4]
        return carry

    lax.fori_loop(0, TILES, composite, 0)

    lane = iota((TILES, COLS), 1)
    in_tile = (lane >> 4) == tile_row
    for y in range(16):
        index = (lane & 15) + 16 * (y % 8)
        for c in range(3):
            half = 128 * (y // 8)
            source = tile_rad_ref[c * TILES : (c + 1) * TILES, half : half + 128]
            line = jnp.sum(jnp.where(in_tile, lane_gather(source, index), 0.0), axis=0, keepdims=True)
            strips_ref[1, c, y : y + 1, :] = line

    @pl.when(me < n - 1)
    def _():
        strip_copy(after, 0).start()

    @pl.when(me > 0)
    def _():
        strip_copy(before, 1).start()

    rad_ref[0] = strips_ref[1]

    channel = iota((16, COLS), 0)
    of_colour = [lax.rem(channel, 3) == c for c in range(3)]
    bracket = channel // 3
    exposure = jnp.zeros((16, COLS), F32)
    for b in range(5):
        exposure = jnp.where(bracket == b, expo_ref[0, b], exposure)

    @pl.when(me > 0)
    def _():
        strip_copy(before, 0).wait_recv()

    @pl.when(me < n - 1)
    def _():
        strip_copy(after, 1).wait_recv()

    def tone(row, carry):
        strip = row // ROWS
        y = lax.rem(row, ROWS)
        lines = [strips_ref[strip, c, pl.ds(y, 1), :] for c in range(3)]
        scaled = exposure * jnp.where(
            of_colour[0], lines[0], jnp.where(of_colour[1], lines[1], lines[2])
        )
        mapped = scaled / (1.0 + scaled)
        rows = pl.ds(pl.multiple_of(row * 16, 16), 16)
        p_ref[rows, :] = mapped
        pp_ref[rows, :] = mapped * mapped
        pt_ref[rows, :] = mapped * t_ref[rows, :]
        return carry

    lax.fori_loop(FIRST - 5, FIRST + MAPS + 5, tone, 0)

    def similarity_row(i, carry):
        row = FIRST + i
        rows = pl.ds(pl.multiple_of(i * 16, 16), 16)
        mean_p = along_columns(along_rows(p_ref, row), taps)
        square_p = along_columns(along_rows(pp_ref, row), taps)
        cross = along_columns(along_rows(pt_ref, row), taps)
        mean_t = mt_ref[rows, :]
        both = mean_p * mean_t
        n1 = 2.0 * both + FLOOR_MEAN
        n2 = 2.0 * (cross - both) + FLOOR_VAR
        d1 = mean_p * mean_p + mean_t * mean_t + FLOOR_MEAN
        d2 = (square_p - mean_p * mean_p) + (btt_ref[rows, :] - mean_t * mean_t) + FLOOR_VAR
        inside = ((row >= ROWS) | (me > 0)) & ((row < 2 * ROWS) | (me < n - 1))
        share = jnp.where(inside, 1.0, 0.0) / (d1 * d2)
        similar = n1 * n2 * share
        gpt_ref[rows, :] = -2.0 * n1 * share
        by_d2 = similar / d2
        gpp_ref[rows, :] = by_d2
        gm_ref[rows, :] = 2.0 * (
            mean_t * (n1 - n2) * share + mean_p * (similar / d1 - by_d2)
        )
        return carry

    lax.fori_loop(0, MAPS, similarity_row, 0)

    def radiance_row(y, carry):
        own = pl.ds(pl.multiple_of((y + ROWS) * 16, 16), 16)
        mapped = p_ref[own, :]
        wanted = t_ref[own, :]
        slope = along_columns(along_rows(gm_ref, y + 5), taps)
        slope = slope + 2.0 * mapped * along_columns(along_rows(gpp_ref, y + 5), taps)
        slope = slope + wanted * along_columns(along_rows(gpt_ref, y + 5), taps)
        slope = slope + 1.6 * (mapped - wanted)
        rest = 1.0 - mapped
        slope = slope * exposure * (rest * rest)
        for c in range(3):
            line = jnp.sum(jnp.where(of_colour[c], slope, 0.0), axis=0, keepdims=True)
            gimg_ref[pl.ds(c * ROWS + y, 1), :] = line
        return carry

    lax.fori_loop(0, ROWS, radiance_row, 0)

    spread_index = 16 * tile_row + (lane & 15)
    for c in range(3):
        for half in range(2):
            total = jnp.zeros((TILES, COLS), F32)
            for y in range(8):
                row = c * ROWS + half * 8 + y
                source = jnp.broadcast_to(gimg_ref[row : row + 1, :], (TILES, COLS))
                total = jnp.where((lane >> 4) == y, lane_gather(source, spread_index), total)
            gtile_ref[c * TILES : (c + 1) * TILES, 128 * half : 128 * half + 128] = total

    def composite_back(j, carry):
        ox, oy, a, b, c_ = [splat_row(f, j) for f in range(5)]
        colours = jnp.concatenate([splat_row(6 + c, j) for c in range(3)], axis=0)
        colour_top = colours.astype(BF16).astype(F32)
        slopes = jnp.concatenate(
            [gtile_ref[pl.ds(c * TILES + j, 1), :] for c in range(3)], axis=0
        )
        slope_top = slopes.astype(BF16).astype(F32)
        left = jnp.concatenate(
            [slope_top, slopes - slope_top, slope_top, jnp.zeros((7, LIST), F32)], axis=0
        )
        right = jnp.concatenate(
            [colour_top, colour_top, colours - colour_top, jnp.zeros((7, LIST), F32)], axis=0
        )
        deriv_ref[...] = dot(left.T.astype(BF16), right.astype(BF16))
        for y in range(16):
            rows = pixel_rows(j, y)
            value = deriv_ref[y * 16 : y * 16 + 16, :] * weight_ref[rows, :]
            weight_ref[rows, :] = value
            top, low = parts(value)
            pair_ref[y * 16 : y * 16 + 16, 0:LIST] = top
            pair_ref[y * 16 : y * 16 + 16, LIST : 2 * LIST] = low
        deriv_ref[...] = dot(pair_ref[...], later)
        dx = column_x - ox
        dxx = dx * dx
        zero = jnp.zeros((ROWS, LIST), F32)
        m0, mx, mxx = zero, zero, zero
        my, mxy, myy = zero, zero, zero
        for y in range(16):
            rows = pixel_rows(j, y)
            dy = (y + 0.5 - 8.0) - oy
            q = weight_ref[rows, :] - deriv_ref[y * 16 : y * 16 + 16, :] * cover_ref[rows, :]
            qx = q * dx
            qy = q * dy
            m0 = m0 + q
            mx = mx + qx
            my = my + qy
            mxx = mxx + q * dxx
            mxy = mxy + qx * dy
            myy = myy + qy * dy
        m0, mx, my, mxx, mxy, myy = [
            jnp.sum(m, axis=0, keepdims=True) for m in (m0, mx, my, mxx, mxy, myy)
        ]
        tile_rows = pl.ds(pl.multiple_of(j * 256, 256), 256)
        packed = left.astype(BF16)
        by_colour = dot(packed, top_ref[tile_rows, :]) + dot(packed, low_ref[tile_rows, :])
        rows = [
            a * mx + b * my,
            b * mx + c_ * my,
            -0.5 * mxx,
            -mxy,
            -0.5 * myy,
            m0 / splat_row(5, j),
        ] + [by_colour[c : c + 1] + by_colour[c + 3 : c + 4] for c in range(3)]
        lanes = pl.ds(pl.multiple_of(j * LIST, LIST), LIST)
        mask = slot_mask_ref[:, lanes]
        for f in range(SPLAT):
            top = rows[f].astype(BF16).astype(F32)
            for k, part in enumerate((top, rows[f] - top)):
                at = (k * SPLAT + f) * halves
                slot_left_ref[at : at + halves, :] = (
                    jnp.broadcast_to(part, (halves, LIST)).astype(BF16) * mask
                )
        update = dot_nt(slot_left_ref[...], slot_one_ref[:, lanes])

        @pl.when(j == 0)
        def _():
            slot_sum_ref[...] = update

        @pl.when(j > 0)
        def _():
            slot_sum_ref[...] = slot_sum_ref[...] + update

        return carry

    lax.fori_loop(0, TILES, composite_back, 0)

    count = SPLAT * halves
    for side in range(2):
        lanes = slice(side * COLS, side * COLS + COLS)
        sgrad_ref[side * count : (side + 1) * count, :] = (
            slot_sum_ref[0:count, lanes] + slot_sum_ref[count : 2 * count, lanes]
        )

    def send_back(step, carry):
        block = lax.rem(my_group + step, groups)
        for i in range(group):
            peer = block * group + i
            first = (i % 2) * count + block * (group // 2) + i // 2
            back_ref[peer] = sgrad_ref[pl.ds(first, SPLAT, stride=halves), :]
        for i in range(group):
            peer = block * group + lax.rem(me + i, group)

            @pl.when(peer != me)
            def _():
                back_copy(peer, me).start()

        return carry

    lax.fori_loop(0, groups, send_back, 0)
    ret_ref[me] = back_ref[me]

    own_sum_ref[...] = jnp.zeros_like(own_sum_ref)

    def add_group(step, carry):
        block = lax.rem(my_group + groups - step, groups)
        for i in range(group):
            sender = block * group + i

            @pl.when(sender != me)
            def _():
                back_copy(sender, sender).wait_recv()

        for i in range(group):
            sender = block * group + i
            mask = own_mask_ref[:, pl.ds(pl.multiple_of(sender * COLS, COLS), COLS)]
            message = ret_ref[sender]
            top = message.astype(BF16).astype(F32)
            for k, part in enumerate((top, message - top)):
                for f in range(SPLAT):
                    at = (k * SPLAT + f) * 16
                    own_left_ref[at : at + 16, i * COLS : (i + 1) * COLS] = (
                        jnp.broadcast_to(part[f : f + 1], (16, COLS)).astype(BF16) * mask
                    )
        lanes = pl.ds(pl.multiple_of(block * group * COLS, COLS), group * COLS)
        own_sum_ref[...] = own_sum_ref[...] + dot_nt(own_left_ref[...], own_one_ref[:, lanes])
        return carry

    lax.fori_loop(0, groups, add_group, 0)
    for f in range(SPLAT):
        for side in range(2):
            lanes = slice(side * COLS, side * COLS + COLS)
            low = (SPLAT + f) * 16
            gown_ref[pl.ds(f * HIGH + side, 16, stride=2), :] = (
                own_sum_ref[f * 16 : f * 16 + 16, lanes] + own_sum_ref[low : low + 16, lanes]
            )

    def view_copy(peer, slot):
        return pltpu.make_async_remote_copy(
            src_ref=gown_ref,
            dst_ref=gall_ref.at[slot],
            send_sem=v_send.at[peer],
            recv_sem=v_recv.at[slot],
            device_id={"view": peer},
            device_id_type=MESH,
        )

    for i in range(1, nv):
        view_copy(lax.rem(mv + i, nv), mv).start()
    gall_ref[mv] = gown_ref[...]

    def drain(i, carry):
        peer = lax.rem(me + i, n)
        forward_copy(peer, me).wait_send()
        back_copy(peer, me).wait_send()
        return carry

    lax.fori_loop(1, n, drain, 0)

    @pl.when(me < n - 1)
    def _():
        target_copy(after, 0).wait_send()
        strip_copy(after, 0).wait_send()

    @pl.when(me > 0)
    def _():
        target_copy(before, 1).wait_send()
        strip_copy(before, 1).wait_send()

    for i in range(1, nv):
        peer = lax.rem(mv + i, nv)
        view_copy(peer, mv).wait_send()
        view_copy(peer, peer).wait_recv()


def pull_back_kernel(nv, gauss_ref, gall_ref, rad_ref, grad_ref, radiance_ref, wide_ref, sum_ref):
    radiance_ref[...] = rad_ref[...]
    spread_rows(gauss_ref, wide_ref)

    def one_view(v, carry):
        camera = [
            jnp.broadcast_to(gall_ref[v, pl.ds(SPLAT * HIGH + i, 1), :], (8, COLS)) for i in range(5)
        ]
        rotation = camera_rotation(camera)

        def one_chunk(i, inner):
            def rows(f):
                return pl.ds(pl.multiple_of(f * HIGH + i * 8, 8), 8)

            params = [wide_ref[rows(f), :] for f in range(FEAT)]
            slopes = [gall_ref[v, rows(f), :] for f in range(SPLAT)]
            _, pull = jax.vjp(lambda values: project(values, camera, rotation), params)
            (grads,) = pull(slopes)
            for f in range(FEAT):
                sum_ref[rows(f), :] = jnp.where(v == 0, 0.0, sum_ref[rows(f), :]) + grads[f]
            return inner

        return lax.fori_loop(0, HIGH // 8, one_chunk, carry)

    lax.fori_loop(0, nv, one_view, 0)

    def collect(h, carry):
        lanes = pl.ds(pl.multiple_of(h * COLS, COLS), COLS)
        for first in range(0, FEAT, 8):
            size = min(8, FEAT - first)
            grad_ref[first : first + size, lanes] = sum_ref[pl.ds(first * HIGH + h, size, stride=HIGH), :]
        return carry

    lax.fori_loop(0, HIGH, collect, 0)


def shards(n, nv, gaussians, send_index, tile_list, tile_length, camera, exposure, target):
    vmem = pl.BlockSpec(memory_space=pltpu.VMEM)
    smem = pl.BlockSpec(memory_space=pltpu.SMEM)
    halves = max(16, n // 2)
    group = min(8, n)

    def scratch(shape, dtype=F32):
        return pltpu.VMEM(shape, dtype)

    pixels = TILES * 256
    scratches = [
        scratch((64 * HIGH, COLS)),
        scratch((SPLAT * HIGH, COLS)),
        scratch((SPLAT * group, COLS)),
        scratch((n, SPLAT, COLS)),
        scratch((n, SPLAT, COLS)),
        scratch(((SPLAT + 1) * TILES, LIST)),
        scratch((pixels, LIST)),
        scratch((pixels, LIST)),
        scratch((pixels, LIST), BF16),
        scratch((pixels, LIST), BF16),
        scratch((LIST, 2 * LIST), BF16),
        scratch((LIST, LIST)),
        scratch((3 * TILES, LIST)),
        scratch((3, 3, ROWS, COLS)),
        scratch((2, CHANNELS, ROWS, COLS)),
        scratch((48 * 16, COLS)),
        scratch((48 * 16, COLS)),
        scratch((48 * 16, COLS)),
        scratch((48 * 16, COLS)),
        scratch((48 * 16, COLS)),
        scratch((MAPS * 16, COLS)),
        scratch((MAPS * 16, COLS)),
        scratch((MAPS * 16, COLS)),
        scratch((MAPS * 16, COLS)),
        scratch((MAPS * 16, COLS)),
        scratch((3 * ROWS, COLS)),
        scratch((3 * TILES, LIST)),
        scratch((2 * SPLAT * halves, COLS)),
        scratch((256, TILES * LIST), BF16),
        scratch((halves, TILES * LIST), BF16),
        scratch((256, n * COLS), BF16),
        scratch((16, n * COLS), BF16),
        scratch((2 * SPLAT * halves, LIST), BF16),
        scratch((2 * SPLAT * halves, 256)),
        scratch((n, SPLAT, COLS)),
        scratch((n, SPLAT, COLS)),
        scratch((2 * SPLAT * 16, group * COLS), BF16),
        scratch((2 * SPLAT * 16, 256)),
        scratch((SPLAT * HIGH + 8, COLS)),
    ]
    sems = [pltpu.SemaphoreType.DMA((k,)) for k in (n, n, n, n, 2, 2, 2, 2, nv, nv)]
    gathered, strip = pl.pallas_call(
        functools.partial(step_kernel, n, nv),
        out_shape=(
            jax.ShapeDtypeStruct((nv, SPLAT * HIGH + 8, COLS), F32),
            jax.ShapeDtypeStruct((1, 3, ROWS, COLS), F32),
        ),
        in_specs=[vmem, vmem, vmem, smem, smem, smem, vmem],
        out_specs=(vmem, vmem),
        scratch_shapes=scratches + sems,
        compiler_params=pltpu.CompilerParams(
            collective_id=0, has_side_effects=True, vmem_limit_bytes=50 * 2**20
        ),
        name="splat_step",
    )(gaussians, send_index, tile_list, tile_length, camera, exposure, target)
    return pl.pallas_call(
        functools.partial(pull_back_kernel, nv),
        out_shape=(
            jax.ShapeDtypeStruct((FEAT, HIGH * COLS), F32),
            jax.ShapeDtypeStruct((1, 3, ROWS, COLS), F32),
        ),
        in_specs=[vmem, vmem, vmem],
        out_specs=(vmem, vmem),
        scratch_shapes=[scratch((64 * HIGH, COLS)), scratch((64 * HIGH, COLS))],
        compiler_params=pltpu.CompilerParams(vmem_limit_bytes=32 * 2**20),
        name="pull_back",
    )(gaussians, gathered, strip)


def solution(mesh):
    placed = (
        P(None, "gs"),
        P("view", "gs", None),
        P("view", "gs", None),
        P("view", "gs"),
        P("view", None),
        P("view", None),
        P("view", None, "gs", None),
    )
    return jax.shard_map(
        functools.partial(shards, mesh.shape["gs"], mesh.shape["view"]),
        mesh=mesh,
        in_specs=placed,
        out_specs=(P(None, "gs"), P("view", None, "gs", None)),
        check_vma=False,
    )
```

profile of v0, /device:TPU:1, one launch (start us, length us, event | category | flops | bytes accessed | tf_op | source)
XLA Modules:
  0.0 84.5 jit_solution(11032497348242785586)
XLA Ops:
  0.6 0.0 copy-start
  0.6 1.2 %copy-done = f32[59,4096]{1,0:T(8,128)S(1)} copy-done((f32[59,4096]{1,0:T(8,128)S(1)}, f32[59,4096]{1,0:T(8,128)}, u32[]{:S(2)}) %copy-start) | copy-done | bytes 966680
  1.9 0.0 copy-start.1
  1.9 0.9 %copy-done.1 = f32[1,15,16,128]{3,2,1,0:T(8,128)S(1)} copy-done((f32[1,15,16,128]{3,2,1,0:T(8,128)S(1)}, f32[1,15,16,128]{3,2,1,0:T(8,128)}, u32[]{:S(2)}) %copy-start.1) | copy-done | bytes 122904
  2.8 0.0 copy-start.2
  2.8 0.8 copy-done.2
  3.5 0.0 copy-start.3
  3.5 0.7 copy-done.3
  4.2 0.0 copy-start.4
  4.2 0.7 copy-done.4
  4.9 0.0 copy-start.5
  4.9 0.7 copy-done.5
  5.5 0.0 copy-start.6
  5.5 0.7 copy-done.6
  6.2 72.1 %splat_step.1 = (f32[4,296,128]{2,1,0:T(8,128)S(1)}, f32[1,3,16,128]{3,2,1,0:T(8,128)S(1)}) custom-call(f32[59,4096]{1,0:T(8,128)S(1)} %copy-done, s32[1,64,128]{2,1,0:T(8,128)S(1)} %copy-done.2, s32[1,8,256]{2,1,0:T(8,128)S(1)} %copy-done.3, s32[1,8]{1,0:T(1,128)S(1)} %copy-done.4, f32[1,5]{1,0:T(1,128)S(1)} %copy-done.5, f32[1,5]{1,0:T(1,128)S(1)} %copy-done.6, ...), custom_call_target="tpu_custom_call" | custom-call | tf_op jit(solution)/shard_map/splat_step/pallas_call | solution.py:908
  78.3 6.2 %pull_back.1 = (f32[59,4096]{1,0:T(8,128)}, f32[1,3,16,128]{3,2,1,0:T(8,128)}) custom-call(f32[59,4096]{1,0:T(8,128)S(1)} %copy-done, f32[4,296,128]{2,1,0:T(8,128)S(1)} %get-tuple-element.4.gall_ref, f32[1,3,16,128]{3,2,1,0:T(8,128)S(1)} %get-tuple-element.5.rad_ref), custom_call_target="tpu_custom_call" | custom-call | tf_op jit(solution)/shard_map/pull_back/pallas_call | solution.py:922
Async XLA Ops:
  0.6 1.2 %copy-start = (f32[59,4096]{1,0:T(8,128)S(1)}, f32[59,4096]{1,0:T(8,128)}, u32[]{:S(2)}) copy-start(f32[59,4096]{1,0:T(8,128)} %gauss_ref.3) | copy-start | bytes 2899972
  1.9 0.9 %copy-start.1 = (f32[1,15,16,128]{3,2,1,0:T(8,128)S(1)}, f32[1,15,16,128]{3,2,1,0:T(8,128)}, u32[]{:S(2)}) copy-start(f32[1,15,16,128]{3,2,1,0:T(8,128)} %target_ref.1) | copy-start | bytes 368644
  2.8 0.8 copy-start.2
  3.5 0.7 copy-start.3
  4.2 0.7 copy-start.4
  4.9 0.7 copy-start.5
  5.5 0.7 copy-start.6
where the time goes:
time: 84.8 us; the launch traced here: 84.5 us
  Pallas kernels  78.3 us (92%)
  local copies, waits for them, and re-layouts  5.54 us (7%)
    pallas_call x1, Pallas kernels, shards(): pl.pallas_call(functools.partial(step_kernel, n, nv), out_shape=(jax.Shap...  72.1 us
    pallas_call x1, Pallas kernels, shards(): pl.pallas_call(functools.partial(pull_back_kernel, nv), out_shape=(jax.Sh...  6.2 us
    unnamed x14, local copies, waits for them, and re-layouts  5.54 us

commit v1 on v0

--- a/solution.py
+++ b/solution.py
@@ -45,6 +45,7 @@
 COLS = 128
 CHANNELS = 15
 FIRST = 11
+JAC = 45
 MAPS = 26
 
 
@@ -198,6 +199,15 @@
 def step_kernel(
     n,
     nv,
+    gauss_hbm,
+    send_hbm,
+    list_hbm,
+    len_hbm,
+    cam_hbm,
+    expo_hbm,
+    target_hbm,
+    wide_grad_ref,
+    rad_ref,
     gauss_ref,
     send_ref,
     list_ref,
@@ -205,8 +215,6 @@
     cam_ref,
     expo_ref,
     target_ref,
-    gall_ref,
-    rad_ref,
     wide_ref,
     table_ref,
     pick_ref,
@@ -245,7 +253,10 @@
     ret_ref,
     own_left_ref,
     own_sum_ref,
-    gown_ref,
+    gall_ref,
+    cams_ref,
+    turn_ref,
+    jac_ref,
     f_send,
     f_recv,
     b_send,
@@ -256,6 +267,9 @@
     h_recv,
     v_send,
     v_recv,
+    c_send,
+    c_recv,
+    in_sem,
 ):
     me = lax.axis_index("gs")
     mv = lax.axis_index("view")
@@ -265,6 +279,23 @@
     groups = n // group
     halves = slot_mask_ref.shape[0]
 
+    loads = [
+        pltpu.make_async_copy(source, place, in_sem.at[i])
+        for i, (source, place) in enumerate(
+            [
+                (gauss_hbm, gauss_ref),
+                (cam_hbm, cam_ref),
+                (send_hbm, send_ref),
+                (target_hbm, target_ref),
+                (list_hbm, list_ref),
+                (len_hbm, len_ref),
+                (expo_hbm, expo_ref),
+            ]
+        )
+    ]
+    for load in loads:
+        load.start()
+
     barrier = pltpu.get_barrier_semaphore()
 
     def greet(i, carry):
@@ -279,8 +310,10 @@
             barrier, inc=1, device_id={"view": lax.rem(mv + i, nv)}, device_id_type=MESH
         )
 
+    loads[0].wait()
+    loads[1].wait()
     spread_rows(gauss_ref, wide_ref)
-    camera = [jnp.full((8, COLS), cam_ref[0, i], F32) for i in range(5)]
+    camera = [jnp.broadcast_to(cam_ref[0:1, i : i + 1], (8, COLS)) for i in range(5)]
     rotation = camera_rotation(camera)
 
     def project_rows(i, carry):
@@ -291,11 +324,13 @@
             table_ref[pl.ds(pl.multiple_of(f * HIGH + i * 8, 8), 8), :] = value
         return carry
 
-    lax.fori_loop(0, HIGH // 8, project_rows, 0)
-    for i in range(5):
-        gown_ref[SPLAT * HIGH + i : SPLAT * HIGH + i + 1, :] = camera[i][0:1]
-    gown_ref[SPLAT * HIGH + 5 : SPLAT * HIGH + 8, :] = jnp.zeros((3, COLS), F32)
-
+    lax.fori_loop(0, HIGH // 8, project_rows, 0, unroll=4)
+    cams_ref[mv] = jnp.concatenate(
+        [camera[i][0:1] for i in range(5)] + [jnp.zeros((3, COLS), F32)], axis=0
+    )
+
+    for load in loads[2:]:
+        load.wait()
     pl.semaphore_wait(barrier, n - 1 + nv - 1)
 
     def target_copy(peer, side):
@@ -318,6 +353,16 @@
             device_id_type=MESH,
         )
 
+    def camera_copy(peer, slot):
+        return pltpu.make_async_remote_copy(
+            src_ref=cams_ref.at[mv],
+            dst_ref=cams_ref.at[slot],
+            send_sem=c_send.at[peer],
+            recv_sem=c_recv.at[slot],
+            device_id={"view": peer},
+            device_id_type=MESH,
+        )
+
     @pl.when(me < n - 1)
     def _():
         target_copy(after, 0).start()
@@ -348,8 +393,12 @@
 
     my_group = me // group
 
+    def shift_of(step):
+        reach = groups // 2 - (step + 1) // 2
+        return jnp.where(step % 2 == 1, reach, lax.rem(groups - reach, groups))
+
     def gather_group(step, carry):
-        block = lax.rem(my_group + step, groups)
+        block = lax.rem(my_group + shift_of(step), groups)
         index = send_ref[0, pl.ds(pl.multiple_of(block * group, group), group), :]
         high = index >> 7
         low = index & 127
@@ -363,7 +412,7 @@
             return tuple(new)
 
         totals = lax.fori_loop(
-            0, HIGH, one, tuple(jnp.zeros((group, COLS), F32) for _ in range(SPLAT)), unroll=4
+            0, HIGH, one, tuple(jnp.zeros((group, COLS), F32) for _ in range(SPLAT)), unroll=8
         )
         for f in range(SPLAT):
             pick_ref[f * group : (f + 1) * group, :] = totals[f]
@@ -381,6 +430,8 @@
 
     lax.fori_loop(0, groups, gather_group, 0)
     recv_ref[me] = out_ref[me]
+    for i in range(1, nv):
+        camera_copy(lax.rem(mv + i, nv), mv).start()
 
     def own_factors(r, carry):
         index = send_ref[0, pl.ds(r, 1), :]
@@ -389,7 +440,7 @@
         own_mask_ref[:, lanes] = jnp.where(iota((16, COLS), 0) == (index >> 8), 1.0, 0.0).astype(BF16)
         return carry
 
-    lax.fori_loop(0, n, own_factors, 0)
+    lax.fori_loop(0, n, own_factors, 0, unroll=8)
 
     def slot_factors(j, carry):
         index = list_ref[0, pl.ds(j, 1), :]
@@ -400,7 +451,7 @@
         )
         return carry
 
-    lax.fori_loop(0, TILES, slot_factors, 0)
+    lax.fori_loop(0, TILES, slot_factors, 0, unroll=8)
 
     @pl.when(me == 0)
     def _():
@@ -437,7 +488,7 @@
         tt_ref[rows, :] = t_ref[rows, :] * t_ref[rows, :]
         return carry
 
-    lax.fori_loop(FIRST - 5, FIRST + MAPS + 5, square_target, 0)
+    lax.fori_loop(FIRST - 5, FIRST + MAPS + 5, square_target, 0, unroll=4)
 
     def target_maps(i, carry):
         rows = pl.ds(pl.multiple_of(i * 16, 16), 16)
@@ -445,13 +496,13 @@
         btt_ref[rows, :] = along_columns(along_rows(tt_ref, FIRST + i), taps)
         return carry
 
-    lax.fori_loop(0, MAPS, target_maps, 0)
+    lax.fori_loop(0, MAPS, target_maps, 0, unroll=26)
 
     owner = [list_ref[0, :, 128 * h : 128 * h + 128] >> 7 for h in range(2)]
     place = [list_ref[0, :, 128 * h : 128 * h + 128] & 127 for h in range(2)]
 
     def take_group(step, totals):
-        block = lax.rem(my_group + groups - step, groups)
+        block = lax.rem(my_group + groups - shift_of(step), groups)
         for i in range(group):
             sender = block * group + i
 
@@ -478,7 +529,7 @@
     tile_row = iota((TILES, COLS), 0)
     length = jnp.zeros((TILES, COLS), I32)
     for j in range(TILES):
-        length = jnp.where(tile_row == j, len_ref[0, j], length)
+        length = jnp.where(tile_row == j, len_ref[0:1, j : j + 1], length)
     for f in range(SPLAT):
         for h in range(2):
             splat_ref[f * TILES : (f + 1) * TILES, 128 * h : 128 * h + 128] = totals[2 * f + h]
@@ -537,7 +588,7 @@
             tile_rad_ref[pl.ds(c * TILES + j, 1), :] = seen[c : c + 1] + seen[c + 3 : c + 4]
         return carry
 
-    lax.fori_loop(0, TILES, composite, 0)
+    lax.fori_loop(0, TILES, composite, 0, unroll=8)
 
     lane = iota((TILES, COLS), 1)
     in_tile = (lane >> 4) == tile_row
@@ -564,7 +615,7 @@
     bracket = channel // 3
     exposure = jnp.zeros((16, COLS), F32)
     for b in range(5):
-        exposure = jnp.where(bracket == b, expo_ref[0, b], exposure)
+        exposure = jnp.where(bracket == b, expo_ref[0:1, b : b + 1], exposure)
 
     @pl.when(me > 0)
     def _():
@@ -588,7 +639,7 @@
         pt_ref[rows, :] = mapped * t_ref[rows, :]
         return carry
 
-    lax.fori_loop(FIRST - 5, FIRST + MAPS + 5, tone, 0)
+    lax.fori_loop(FIRST - 5, FIRST + MAPS + 5, tone, 0, unroll=36)
 
     def similarity_row(i, carry):
         row = FIRST + i
@@ -613,7 +664,7 @@
         )
         return carry
 
-    lax.fori_loop(0, MAPS, similarity_row, 0)
+    lax.fori_loop(0, MAPS, similarity_row, 0, unroll=26)
 
     def radiance_row(y, carry):
         own = pl.ds(pl.multiple_of((y + ROWS) * 16, 16), 16)
@@ -630,7 +681,7 @@
             gimg_ref[pl.ds(c * ROWS + y, 1), :] = line
         return carry
 
-    lax.fori_loop(0, ROWS, radiance_row, 0)
+    lax.fori_loop(0, ROWS, radiance_row, 0, unroll=16)
 
     spread_index = 16 * tile_row + (lane & 15)
     for c in range(3):
@@ -717,7 +768,7 @@
 
         return carry
 
-    lax.fori_loop(0, TILES, composite_back, 0)
+    lax.fori_loop(0, TILES, composite_back, 0, unroll=8)
 
     count = SPLAT * halves
     for side in range(2):
@@ -727,7 +778,7 @@
         )
 
     def send_back(step, carry):
-        block = lax.rem(my_group + step, groups)
+        block = lax.rem(my_group + shift_of(step), groups)
         for i in range(group):
             peer = block * group + i
             first = (i % 2) * count + block * (group // 2) + i // 2
@@ -744,10 +795,89 @@
     lax.fori_loop(0, groups, send_back, 0)
     ret_ref[me] = back_ref[me]
 
+    for i in range(1, nv):
+        peer = lax.rem(mv + i, nv)
+        camera_copy(peer, peer).wait_recv()
+    for v in range(nv):
+        angles = [jnp.broadcast_to(cams_ref[v, i : i + 1, :], (8, COLS)) for i in range(5)]
+        turn = camera_rotation(angles)
+        shift = [0.15 * angles[3], 0.15 * angles[4], 6.0]
+        flat = [jnp.broadcast_to(turn[i][k], (8, COLS)) for i in range(3) for k in range(3)]
+        flat += [sum((turn[i][k] * shift[i] for i in range(3))) for k in range(3)]
+        for k in range(12):
+            turn_ref[v, 8 * k : 8 * k + 8, :] = flat[k]
+
+    def chunk_rows(f, i):
+        return pl.ds(pl.multiple_of(f * HIGH + i * 8, 8), 8)
+
+    def turn_of(v):
+        flat = [turn_ref[v, 8 * k : 8 * k + 8, :] for k in range(12)]
+        return [flat[0:3], flat[3:6], flat[6:9]], flat[9:12]
+
+    def prepare(i, carry):
+        position = [wide_ref[chunk_rows(f, i), :] for f in range(3)]
+        stretch = [jnp.exp(wide_ref[chunk_rows(3 + k, i), :]) for k in range(3)]
+        orient = quaternion_matrix(*[wide_ref[chunk_rows(6 + k, i), :] for k in range(4)])
+        for v in range(nv):
+            turn, away = turn_of(v)
+            shift = [
+                0.15 * jnp.broadcast_to(cams_ref[v, 3:4, :], (8, COLS)),
+                0.15 * jnp.broadcast_to(cams_ref[v, 4:5, :], (8, COLS)),
+                6.0,
+            ]
+            viewed = [
+                sum((turn[r][k] * position[k] for k in range(3))) + shift[r] for r in range(3)
+            ]
+            inverse_z = 1.0 / viewed[2]
+            slant_x = viewed[0] * inverse_z
+            slant_y = viewed[1] * inverse_z
+            focal_z = FOCAL * inverse_z
+            row_x = [focal_z * (turn[0][k] - slant_x * turn[2][k]) for k in range(3)]
+            row_y = [focal_z * (turn[1][k] - slant_y * turn[2][k]) for k in range(3)]
+            image_x = [
+                sum((row_x[r] * orient[r][k] for r in range(3))) * stretch[k] for k in range(3)
+            ]
+            image_y = [
+                sum((row_y[r] * orient[r][k] for r in range(3))) * stretch[k] for k in range(3)
+            ]
+            cov_xx = sum((e * e for e in image_x)) + DILATE
+            cov_yy = sum((e * e for e in image_y)) + DILATE
+            cov_xy = sum((image_x[k] * image_y[k] for k in range(3)))
+            share = 1.0 / (cov_xx * cov_yy - cov_xy * cov_xy)
+            toward = [position[k] + away[k] for k in range(3)]
+            closeness = 1.0 / jnp.sqrt(sum((e * e for e in toward)))
+            direction = [e * closeness for e in toward]
+            harmonic, pull = jax.vjp(harmonics, *direction)
+            colours, moves = [], []
+            for c in range(3):
+                factors = [wide_ref[chunk_rows(11 + 3 * l + c, i), :] for l in range(16)]
+                colour = jnp.exp(sum((harmonic[l] * factors[l] for l in range(16))))
+                slope = pull(factors)
+                along = sum((direction[k] * slope[k] for k in range(3)))
+                reach = closeness * colour
+                colours.append(colour)
+                moves += [(slope[k] - direction[k] * along) * reach for k in range(3)]
+            kept = (
+                harmonic[1:]
+                + colours
+                + moves
+                + [cov_yy * share, -cov_xy * share, cov_xx * share]
+                + image_x
+                + image_y
+                + row_x
+                + row_y
+                + [inverse_z, slant_x, slant_y]
+            )
+            for k in range(JAC):
+                jac_ref[v, chunk_rows(k, i), :] = kept[k]
+        return carry
+
+    lax.fori_loop(0, HIGH // 8, prepare, 0)
+
     own_sum_ref[...] = jnp.zeros_like(own_sum_ref)
 
     def add_group(step, carry):
-        block = lax.rem(my_group + groups - step, groups)
+        block = lax.rem(my_group + groups - shift_of(step), groups)
         for i in range(group):
             sender = block * group + i
 
@@ -775,23 +905,119 @@
         for side in range(2):
             lanes = slice(side * COLS, side * COLS + COLS)
             low = (SPLAT + f) * 16
-            gown_ref[pl.ds(f * HIGH + side, 16, stride=2), :] = (
+            gall_ref[mv, pl.ds(f * HIGH + side, 16, stride=2), :] = (
                 own_sum_ref[f * 16 : f * 16 + 16, lanes] + own_sum_ref[low : low + 16, lanes]
             )
 
-    def view_copy(peer, slot):
+    up = lax.rem(mv + 1, nv)
+    down = lax.rem(mv + nv - 1, nv)
+    half = SPLAT * HIGH // 2
+    lower, upper = pl.ds(0, half), pl.ds(half, half)
+
+    def view_copy(slot, rows, peer, k):
         return pltpu.make_async_remote_copy(
-            src_ref=gown_ref,
-            dst_ref=gall_ref.at[slot],
-            send_sem=v_send.at[peer],
-            recv_sem=v_recv.at[slot],
+            src_ref=gall_ref.at[slot, rows],
+            dst_ref=gall_ref.at[slot, rows],
+            send_sem=v_send.at[k],
+            recv_sem=v_recv.at[k],
             device_id={"view": peer},
             device_id_type=MESH,
         )
 
-    for i in range(1, nv):
-        view_copy(lax.rem(mv + i, nv), mv).start()
-    gall_ref[mv] = gown_ref[...]
+    sent = [view_copy(mv, lower, up, 0), view_copy(mv, upper, down, 1)]
+    if nv > 2:
+        sent += [view_copy(mv, upper, up, 2), view_copy(mv, lower, down, 3)]
+    for copy in sent:
+        copy.start()
+    if nv > 2:
+        view_copy(down, lower, up, 0).wait_recv()
+        sent.append(view_copy(down, lower, up, 4))
+        sent[-1].start()
+        view_copy(up, upper, down, 1).wait_recv()
+        sent.append(view_copy(up, upper, down, 5))
+        sent[-1].start()
+        view_copy(down, upper, up, 2).wait_recv()
+        view_copy(up, lower, down, 3).wait_recv()
+        far = lax.rem(mv + 2, nv)
+        view_copy(far, lower, up, 4).wait_recv()
+        view_copy(far, upper, down, 5).wait_recv()
+    else:
+        view_copy(down, lower, up, 0).wait_recv()
+        view_copy(up, upper, down, 1).wait_recv()
+
+    def pull_back(i, carry):
+        stretch = [jnp.exp(wide_ref[chunk_rows(3 + k, i), :]) for k in range(3)]
+        quaternion = [wide_ref[chunk_rows(6 + k, i), :] for k in range(4)]
+        orient, pull = jax.vjp(quaternion_matrix, *quaternion)
+        opacity = 1.0 / (1.0 + jnp.exp(-wide_ref[chunk_rows(10, i), :]))
+        by_position, by_scale, by_orient, by_opacity = [0.0] * 3, [0.0] * 3, [[0.0] * 3] * 3, 0.0
+        by_colour = []
+        for v in range(nv):
+            slope = [gall_ref[v, chunk_rows(f, i), :] for f in range(SPLAT)]
+
+            def kept(k):
+                return jac_ref[v, chunk_rows(k, i), :]
+
+            turn, _ = turn_of(v)
+            a, b, c = [kept(27 + k) for k in range(3)]
+            image_x = [kept(30 + k) for k in range(3)]
+            image_y = [kept(33 + k) for k in range(3)]
+            row_x = [kept(36 + k) for k in range(3)]
+            row_y = [kept(39 + k) for k in range(3)]
+            inverse_z, slant_x, slant_y = [kept(42 + k) for k in range(3)]
+            ab, bb, bc = a * b, b * b, b * c
+            by_xx = -(a * a * slope[2] + ab * slope[3] + bb * slope[4])
+            by_yy = -(bb * slope[2] + bc * slope[3] + c * c * slope[4])
+            by_xy = -(2 * ab * slope[2] + (bb + a * c) * slope[3] + 2 * bc * slope[4])
+            by_x = [2 * by_xx * image_x[k] + by_xy * image_y[k] for k in range(3)]
+            by_y = [2 * by_yy * image_y[k] + by_xy * image_x[k] for k in range(3)]
+            by_scale = [
+                by_scale[k] + by_x[k] * image_x[k] + by_y[k] * image_y[k] for k in range(3)
+            ]
+            by_x = [by_x[k] * stretch[k] for k in range(3)]
+            by_y = [by_y[k] * stretch[k] for k in range(3)]
+            by_orient = [
+                [by_orient[r][k] + row_x[r] * by_x[k] + row_y[r] * by_y[k] for k in range(3)]
+                for r in range(3)
+            ]
+            by_row_x = [sum((orient[r][k] * by_x[k] for k in range(3))) for r in range(3)]
+            by_row_y = [sum((orient[r][k] * by_y[k] for k in range(3))) for r in range(3)]
+            pulled = sum((by_row_x[r] * row_x[r] + by_row_y[r] * row_y[r] for r in range(3)))
+            depth_x = sum((by_row_x[r] * turn[2][r] for r in range(3)))
+            depth_y = sum((by_row_y[r] * turn[2][r] for r in range(3)))
+            by_slant_x = FOCAL * (slope[0] - inverse_z * depth_x)
+            by_slant_y = FOCAL * (slope[1] - inverse_z * depth_y)
+            by_viewed = [
+                by_slant_x * inverse_z,
+                by_slant_y * inverse_z,
+                -inverse_z * (pulled + by_slant_x * slant_x + by_slant_y * slant_y),
+            ]
+            by_position = [
+                by_position[k]
+                + sum((turn[r][k] * by_viewed[r] for r in range(3)))
+                + sum((slope[6 + c_] * kept(18 + 3 * c_ + k) for c_ in range(3)))
+                for k in range(3)
+            ]
+            by_opacity = by_opacity + slope[5]
+            by_colour.append([slope[6 + c_] * kept(15 + c_) for c_ in range(3)])
+        by_quaternion = pull(by_orient)
+        grads = (
+            by_position + by_scale + list(by_quaternion) + [by_opacity * opacity * (1.0 - opacity)]
+        )
+        for f in range(11):
+            wide_grad_ref[chunk_rows(f, i), :] = grads[f]
+        for l in range(16):
+            for c_ in range(3):
+                if l == 0:
+                    total = SH_C0 * sum((by_colour[v][c_] for v in range(nv)))
+                else:
+                    total = sum(
+                        (by_colour[v][c_] * jac_ref[v, chunk_rows(l - 1, i), :] for v in range(nv))
+                    )
+                wide_grad_ref[chunk_rows(11 + 3 * l + c_, i), :] = total
+        return carry
+
+    lax.fori_loop(0, HIGH // 8, pull_back, 0)
 
     def drain(i, carry):
         peer = lax.rem(me + i, n)
@@ -811,51 +1037,31 @@
         target_copy(before, 1).wait_send()
         strip_copy(before, 1).wait_send()
 
+    for copy in sent:
+        copy.wait_send()
     for i in range(1, nv):
-        peer = lax.rem(mv + i, nv)
-        view_copy(peer, mv).wait_send()
-        view_copy(peer, peer).wait_recv()
-
-
-def pull_back_kernel(nv, gauss_ref, gall_ref, rad_ref, grad_ref, radiance_ref, wide_ref, sum_ref):
-    radiance_ref[...] = rad_ref[...]
-    spread_rows(gauss_ref, wide_ref)
-
-    def one_view(v, carry):
-        camera = [
-            jnp.broadcast_to(gall_ref[v, pl.ds(SPLAT * HIGH + i, 1), :], (8, COLS)) for i in range(5)
-        ]
-        rotation = camera_rotation(camera)
-
-        def one_chunk(i, inner):
-            def rows(f):
-                return pl.ds(pl.multiple_of(f * HIGH + i * 8, 8), 8)
-
-            params = [wide_ref[rows(f), :] for f in range(FEAT)]
-            slopes = [gall_ref[v, rows(f), :] for f in range(SPLAT)]
-            _, pull = jax.vjp(lambda values: project(values, camera, rotation), params)
-            (grads,) = pull(slopes)
-            for f in range(FEAT):
-                sum_ref[rows(f), :] = jnp.where(v == 0, 0.0, sum_ref[rows(f), :]) + grads[f]
-            return inner
-
-        return lax.fori_loop(0, HIGH // 8, one_chunk, carry)
-
-    lax.fori_loop(0, nv, one_view, 0)
-
-    def collect(h, carry):
-        lanes = pl.ds(pl.multiple_of(h * COLS, COLS), COLS)
-        for first in range(0, FEAT, 8):
-            size = min(8, FEAT - first)
-            grad_ref[first : first + size, lanes] = sum_ref[pl.ds(first * HIGH + h, size, stride=HIGH), :]
-        return carry
-
-    lax.fori_loop(0, HIGH, collect, 0)
+        camera_copy(lax.rem(mv + i, nv), mv).wait_send()
+
+
+def row_order_kernel(wide_hbm, rad_hbm, grad_ref, radiance_ref, wide_ref, sems):
+    groups = [(first, min(8, FEAT - first)) for first in range(0, FEAT, 8)]
+    loads = [pltpu.make_async_copy(rad_hbm, radiance_ref, sems.at[len(groups)])]
+    for g, (first, size) in enumerate(groups):
+        rows = pl.ds(first * HIGH, size * HIGH)
+        loads.append(pltpu.make_async_copy(wide_hbm.at[rows], wide_ref.at[rows], sems.at[g]))
+    for load in loads:
+        load.start()
+    for g, (first, size) in enumerate(groups):
+        loads[g + 1].wait()
+        for h in range(HIGH):
+            grad_ref[first : first + size, h * COLS : (h + 1) * COLS] = wide_ref[
+                pl.ds(first * HIGH + h, size, stride=HIGH), :
+            ]
+    loads[0].wait()
 
 
 def shards(n, nv, gaussians, send_index, tile_list, tile_length, camera, exposure, target):
     vmem = pl.BlockSpec(memory_space=pltpu.VMEM)
-    smem = pl.BlockSpec(memory_space=pltpu.SMEM)
     halves = max(16, n // 2)
     group = min(8, n)
 
@@ -864,6 +1070,13 @@
 
     pixels = TILES * 256
     scratches = [
+        scratch((FEAT, HIGH * COLS)),
+        scratch((1, n, COLS), I32),
+        scratch((1, TILES, LIST), I32),
+        scratch((1, TILES), I32),
+        scratch((1, 5)),
+        scratch((1, 5)),
+        scratch((1, CHANNELS, ROWS, COLS)),
         scratch((64 * HIGH, COLS)),
         scratch((SPLAT * HIGH, COLS)),
         scratch((SPLAT * group, COLS)),
@@ -902,35 +1115,37 @@
         scratch((n, SPLAT, COLS)),
         scratch((2 * SPLAT * 16, group * COLS), BF16),
         scratch((2 * SPLAT * 16, 256)),
-        scratch((SPLAT * HIGH + 8, COLS)),
+        scratch((nv, SPLAT * HIGH, COLS)),
+        scratch((nv, 8, COLS)),
+        scratch((nv, 12 * 8, COLS)),
+        scratch((nv, JAC * HIGH, COLS)),
     ]
-    sems = [pltpu.SemaphoreType.DMA((k,)) for k in (n, n, n, n, 2, 2, 2, 2, nv, nv)]
-    gathered, strip = pl.pallas_call(
+    sems = [pltpu.SemaphoreType.DMA((k,)) for k in (n, n, n, n, 2, 2, 2, 2, 6, 6, nv, nv, 7)]
+    wide_grad, strip = pl.pallas_call(
         functools.partial(step_kernel, n, nv),
         out_shape=(
-            jax.ShapeDtypeStruct((nv, SPLAT * HIGH + 8, COLS), F32),
+            jax.ShapeDtypeStruct((FEAT * HIGH, COLS), F32),
             jax.ShapeDtypeStruct((1, 3, ROWS, COLS), F32),
         ),
-        in_specs=[vmem, vmem, vmem, smem, smem, smem, vmem],
+        in_specs=[pl.BlockSpec(memory_space=pl.ANY)] * 7,
         out_specs=(vmem, vmem),
         scratch_shapes=scratches + sems,
         compiler_params=pltpu.CompilerParams(
-            collective_id=0, has_side_effects=True, vmem_limit_bytes=50 * 2**20
+            collective_id=0, has_side_effects=True, vmem_limit_bytes=56 * 2**20
         ),
         name="splat_step",
     )(gaussians, send_index, tile_list, tile_length, camera, exposure, target)
     return pl.pallas_call(
-        functools.partial(pull_back_kernel, nv),
+        row_order_kernel,
         out_shape=(
             jax.ShapeDtypeStruct((FEAT, HIGH * COLS), F32),
             jax.ShapeDtypeStruct((1, 3, ROWS, COLS), F32),
         ),
-        in_specs=[vmem, vmem, vmem],
+        in_specs=[pl.BlockSpec(memory_space=pl.ANY)] * 2,
         out_specs=(vmem, vmem),
-        scratch_shapes=[scratch((64 * HIGH, COLS)), scratch((64 * HIGH, COLS))],
-        compiler_params=pltpu.CompilerParams(vmem_limit_bytes=32 * 2**20),
-        name="pull_back",
-    )(gaussians, gathered, strip)
+        scratch_shapes=[scratch((FEAT * HIGH, COLS)), pltpu.SemaphoreType.DMA((9,))],
+        name="row_order",
+    )(wide_grad, strip)
 
 
 def solution(mesh):

time: 84.8 us -> 62.6 us (0.74)
  Pallas kernels: 78.3 us -> 61.7 us
  local copies, waits for them, and re-layouts: 5.54 us -> 0 us
    pallas_call x1, Pallas kernels: 72.1 us -> 59.2 us  [shards(): pl.pallas_call(functools.partial(step_kernel, n, nv), out_shape=(jax.Shap...]
    unnamed x14 -> x0, local copies, waits for them, and re-layouts: 5.54 us -> none
    pallas_call x1, Pallas kernels: 6.2 us -> 2.58 us  [shards(): pl.pallas_call(row_order_kernel, out_shape=(jax.ShapeDtypeStruct((FEAT, H...]
where the time goes in v1:
time: 62.6 us; the launch traced here: 62.4 us
  Pallas kernels  61.7 us (99%)
  between operations  0.64 us (1%)
    pallas_call x1, Pallas kernels, shards(): pl.pallas_call(functools.partial(step_kernel, n, nv), out_shape=(jax.Shap...  59.2 us
    pallas_call x1, Pallas kernels, shards(): pl.pallas_call(row_order_kernel, out_shape=(jax.ShapeDtypeStruct((FEAT, H...  2.58 us

profile of v1, /device:TPU:1, one launch (start us, length us, event | category | flops | bytes accessed | tf_op | source)
XLA Modules:
  0.0 62.4 jit_solution(16414306399981032318)
XLA Ops:
  0.6 59.2 %splat_step.1 = (f32[1888,128]{1,0:T(8,128)}, f32[1,3,16,128]{3,2,1,0:T(8,128)}) custom-call(f32[59,4096]{1,0:T(8,128)} %gauss_hbm.1, s32[1,64,128]{2,1,0:T(8,128)} %send_hbm.1, s32[1,8,256]{2,1,0:T(8,128)} %list_hbm.1, s32[1,8]{1,0:T(1,128)} %len_hbm.1, f32[1,5]{1,0:T(1,128)} %cam_hbm.1, f32[1,5]{1,0:T(1,128)} %expo_hbm.1, f32[1,15,16,128]{3,2,1,0:T(8,128)} %target_hbm.1), custom_call_target="tpu_custom_call" | custom-call | tf_op jit(solution)/shard_map/splat_step/pallas_call | solution.py:1124
  59.8 2.6 %row_order.1 = (f32[59,4096]{1,0:T(8,128)}, f32[1,3,16,128]{3,2,1,0:T(8,128)}) custom-call(f32[1888,128]{1,0:T(8,128)} %get-tuple-element.4.wide_hbm, f32[1,3,16,128]{3,2,1,0:T(8,128)} %get-tuple-element.5.rad_hbm), custom_call_target="tpu_custom_call" | custom-call | tf_op jit(solution)/shard_map/row_order/pallas_call | solution.py:1138

commit v2 on v1

--- a/solution.py
+++ b/solution.py
@@ -169,21 +169,33 @@
     lax.fori_loop(0, HIGH, one, 0)
 
 
-def window_columns():
-    column = iota((1, COLS), 1)
-    taps = []
+def window_band():
+    distance = iota((COLS, COLS), 0) - iota((COLS, COLS), 1)
+    band = jnp.zeros((COLS, COLS), F32)
     for i in range(11):
-        source = column + (i - 5)
-        taps.append(jnp.where((source >= 0) & (source < COLS), WINDOW[i], 0.0))
-    return taps
-
-
-def along_columns(values, taps):
-    total = values * taps[5]
-    for i in range(11):
-        if i != 5:
-            total = total + taps[i] * pltpu.roll(values, (5 - i) % COLS, axis=1)
-    return total
+        band = jnp.where(distance == i - 5, WINDOW[i], band)
+    return band
+
+
+def band_factors():
+    band = window_band()
+    top = band.astype(BF16).astype(F32)
+    middle = (band - top).astype(BF16).astype(F32)
+    low = band - top - middle
+    none = jnp.zeros((COLS, COLS), F32)
+    left = jnp.concatenate([top, top, top, low], axis=0)
+    right = jnp.concatenate([middle, middle, none, none], axis=0)
+    return jnp.concatenate([left, right], axis=1).astype(BF16)
+
+
+def split_three(values, place_ref, rows):
+    top = values.astype(BF16)
+    rest = values - top.astype(F32)
+    middle = rest.astype(BF16)
+    place_ref[rows, 0:COLS] = top
+    place_ref[rows, COLS : 2 * COLS] = middle
+    place_ref[rows, 2 * COLS : 3 * COLS] = (rest - middle.astype(F32)).astype(BF16)
+    place_ref[rows, 3 * COLS : 4 * COLS] = top
 
 
 def along_rows(ref, row):
@@ -240,6 +252,10 @@
     gm_ref,
     gpp_ref,
     gpt_ref,
+    bm_ref,
+    bpp_ref,
+    bpt_ref,
+    split_ref,
     gimg_ref,
     gtile_ref,
     sgrad_ref,
@@ -363,14 +379,6 @@
             device_id_type=MESH,
         )
 
-    @pl.when(me < n - 1)
-    def _():
-        target_copy(after, 0).start()
-
-    @pl.when(me > 0)
-    def _():
-        target_copy(before, 1).start()
-
     def forward_copy(peer, slot):
         return pltpu.make_async_remote_copy(
             src_ref=out_ref.at[peer],
@@ -430,6 +438,14 @@
 
     lax.fori_loop(0, groups, gather_group, 0)
     recv_ref[me] = out_ref[me]
+    @pl.when(me < n - 1)
+    def _():
+        target_copy(after, 0).start()
+
+    @pl.when(me > 0)
+    def _():
+        target_copy(before, 1).start()
+
     for i in range(1, nv):
         camera_copy(lax.rem(mv + i, nv), mv).start()
 
@@ -452,51 +468,6 @@
         return carry
 
     lax.fori_loop(0, TILES, slot_factors, 0, unroll=8)
-
-    @pl.when(me == 0)
-    def _():
-        edge_ref[0] = jnp.zeros((CHANNELS, ROWS, COLS), F32)
-        strips_ref[0] = jnp.zeros((3, ROWS, COLS), F32)
-
-    @pl.when(me == n - 1)
-    def _():
-        edge_ref[1] = jnp.zeros((CHANNELS, ROWS, COLS), F32)
-        strips_ref[2] = jnp.zeros((3, ROWS, COLS), F32)
-
-    @pl.when(me > 0)
-    def _():
-        target_copy(before, 0).wait_recv()
-
-    @pl.when(me < n - 1)
-    def _():
-        target_copy(after, 1).wait_recv()
-
-    for strip in range(3):
-        for ch in range(16):
-            if ch == CHANNELS:
-                value = jnp.zeros((ROWS, COLS), F32)
-            elif strip == 1:
-                value = target_ref[0, ch]
-            else:
-                value = edge_ref[strip // 2, ch]
-            t_ref[pl.ds(strip * 256 + ch, ROWS, stride=16), :] = value
-
-    taps = window_columns()
-
-    def square_target(row, carry):
-        rows = pl.ds(pl.multiple_of(row * 16, 16), 16)
-        tt_ref[rows, :] = t_ref[rows, :] * t_ref[rows, :]
-        return carry
-
-    lax.fori_loop(FIRST - 5, FIRST + MAPS + 5, square_target, 0, unroll=4)
-
-    def target_maps(i, carry):
-        rows = pl.ds(pl.multiple_of(i * 16, 16), 16)
-        mt_ref[rows, :] = along_columns(along_rows(t_ref, FIRST + i), taps)
-        btt_ref[rows, :] = along_columns(along_rows(tt_ref, FIRST + i), taps)
-        return carry
-
-    lax.fori_loop(0, MAPS, target_maps, 0, unroll=26)
 
     owner = [list_ref[0, :, 128 * h : 128 * h + 128] >> 7 for h in range(2)]
     place = [list_ref[0, :, 128 * h : 128 * h + 128] & 127 for h in range(2)]
@@ -608,6 +579,56 @@
     def _():
         strip_copy(before, 1).start()
 
+    @pl.when(me == 0)
+    def _():
+        edge_ref[0] = jnp.zeros((CHANNELS, ROWS, COLS), F32)
+        strips_ref[0] = jnp.zeros((3, ROWS, COLS), F32)
+
+    @pl.when(me == n - 1)
+    def _():
+        edge_ref[1] = jnp.zeros((CHANNELS, ROWS, COLS), F32)
+        strips_ref[2] = jnp.zeros((3, ROWS, COLS), F32)
+
+    @pl.when(me > 0)
+    def _():
+        target_copy(before, 0).wait_recv()
+
+    @pl.when(me < n - 1)
+    def _():
+        target_copy(after, 1).wait_recv()
+
+    for strip in range(3):
+        for ch in range(16):
+            if ch == CHANNELS:
+                value = jnp.zeros((ROWS, COLS), F32)
+            elif strip == 1:
+                value = target_ref[0, ch]
+            else:
+                value = edge_ref[strip // 2, ch]
+            t_ref[pl.ds(strip * 256 + ch, ROWS, stride=16), :] = value
+
+    band = band_factors()
+
+    def square_target(row, carry):
+        rows = pl.ds(pl.multiple_of(row * 16, 16), 16)
+        tt_ref[rows, :] = t_ref[rows, :] * t_ref[rows, :]
+        return carry
+
+    lax.fori_loop(FIRST - 5, FIRST + MAPS + 5, square_target, 0, unroll=4)
+
+    def target_maps(i, carry):
+        rows = pl.ds(pl.multiple_of(i * 16, 16), 16)
+        second = pl.ds(pl.multiple_of((MAPS + i) * 16, 16), 16)
+        split_three(along_rows(t_ref, FIRST + i), split_ref, rows)
+        split_three(along_rows(tt_ref, FIRST + i), split_ref, second)
+        return carry
+
+    lax.fori_loop(0, MAPS, target_maps, 0, unroll=MAPS)
+    count = MAPS * 16
+    for k, maps in enumerate((mt_ref, btt_ref)):
+        both = dot(split_ref[k * count : (k + 1) * count, :], band)
+        maps[...] = both[:, 0:COLS] + both[:, COLS:]
+
     rad_ref[0] = strips_ref[1]
 
     channel = iota((16, COLS), 0)
@@ -617,14 +638,6 @@
     for b in range(5):
         exposure = jnp.where(bracket == b, expo_ref[0:1, b : b + 1], exposure)
 
-    @pl.when(me > 0)
-    def _():
-        strip_copy(before, 0).wait_recv()
-
-    @pl.when(me < n - 1)
-    def _():
-        strip_copy(after, 1).wait_recv()
-
     def tone(row, carry):
         strip = row // ROWS
         y = lax.rem(row, ROWS)
@@ -639,14 +652,39 @@
         pt_ref[rows, :] = mapped * t_ref[rows, :]
         return carry
 
-    lax.fori_loop(FIRST - 5, FIRST + MAPS + 5, tone, 0, unroll=36)
+    lax.fori_loop(ROWS, 2 * ROWS, tone, 0, unroll=ROWS)
+
+    @pl.when(me > 0)
+    def _():
+        strip_copy(before, 0).wait_recv()
+
+    @pl.when(me < n - 1)
+    def _():
+        strip_copy(after, 1).wait_recv()
+
+    lax.fori_loop(FIRST - 5, ROWS, tone, 0, unroll=10)
+    lax.fori_loop(2 * ROWS, FIRST + MAPS + 5, tone, 0, unroll=10)
+
+    def filter_rows(i, carry):
+        rows = pl.ds(pl.multiple_of(i * 16, 16), 16)
+        second = pl.ds(pl.multiple_of((MAPS + i) * 16, 16), 16)
+        third = pl.ds(pl.multiple_of((2 * MAPS + i) * 16, 16), 16)
+        split_three(along_rows(p_ref, FIRST + i), split_ref, rows)
+        split_three(along_rows(pp_ref, FIRST + i), split_ref, second)
+        split_three(along_rows(pt_ref, FIRST + i), split_ref, third)
+        return carry
+
+    lax.fori_loop(0, MAPS, filter_rows, 0, unroll=MAPS)
+    for k, maps in enumerate((gm_ref, gpp_ref, gpt_ref)):
+        both = dot(split_ref[k * count : (k + 1) * count, :], band)
+        maps[...] = both[:, 0:COLS] + both[:, COLS:]
 
     def similarity_row(i, carry):
         row = FIRST + i
         rows = pl.ds(pl.multiple_of(i * 16, 16), 16)
-        mean_p = along_columns(along_rows(p_ref, row), taps)
-        square_p = along_columns(along_rows(pp_ref, row), taps)
-        cross = along_columns(along_rows(pt_ref, row), taps)
+        mean_p = gm_ref[rows, :]
+        square_p = gpp_ref[rows, :]
+        cross = gpt_ref[rows, :]
         mean_t = mt_ref[rows, :]
         both = mean_p * mean_t
         n1 = 2.0 * both + FLOOR_MEAN
@@ -666,13 +704,23 @@
 
     lax.fori_loop(0, MAPS, similarity_row, 0, unroll=26)
 
+    def filter_back(y, carry):
+        for k, source in enumerate((gm_ref, gpp_ref, gpt_ref)):
+            rows = pl.ds(pl.multiple_of((k * ROWS + y) * 16, 16), 16)
+            split_three(along_rows(source, y + 5), split_ref, rows)
+        return carry
+
+    lax.fori_loop(0, ROWS, filter_back, 0, unroll=ROWS)
+    for k, maps in enumerate((bm_ref, bpp_ref, bpt_ref)):
+        both = dot(split_ref[k * ROWS * 16 : (k + 1) * ROWS * 16, :], band)
+        maps[...] = both[:, 0:COLS] + both[:, COLS:]
+
     def radiance_row(y, carry):
         own = pl.ds(pl.multiple_of((y + ROWS) * 16, 16), 16)
         mapped = p_ref[own, :]
         wanted = t_ref[own, :]
-        slope = along_columns(along_rows(gm_ref, y + 5), taps)
-        slope = slope + 2.0 * mapped * along_columns(along_rows(gpp_ref, y + 5), taps)
-        slope = slope + wanted * along_columns(along_rows(gpt_ref, y + 5), taps)
+        rows = pl.ds(pl.multiple_of(y * 16, 16), 16)
+        slope = bm_ref[rows, :] + 2.0 * mapped * bpp_ref[rows, :] + wanted * bpt_ref[rows, :]
         slope = slope + 1.6 * (mapped - wanted)
         rest = 1.0 - mapped
         slope = slope * exposure * (rest * rest)
@@ -929,6 +977,24 @@
         sent += [view_copy(mv, upper, up, 2), view_copy(mv, lower, down, 3)]
     for copy in sent:
         copy.start()
+    def drain(i, carry):
+        peer = lax.rem(me + i, n)
+        forward_copy(peer, me).wait_send()
+        back_copy(peer, me).wait_send()
+        return carry
+
+    lax.fori_loop(1, n, drain, 0)
+
+    @pl.when(me < n - 1)
+    def _():
+        target_copy(after, 0).wait_send()
+        strip_copy(after, 0).wait_send()
+
+    @pl.when(me > 0)
+    def _():
+        target_copy(before, 1).wait_send()
+        strip_copy(before, 1).wait_send()
+
     if nv > 2:
         view_copy(down, lower, up, 0).wait_recv()
         sent.append(view_copy(down, lower, up, 4))
@@ -1019,33 +1085,16 @@
 
     lax.fori_loop(0, HIGH // 8, pull_back, 0)
 
-    def drain(i, carry):
-        peer = lax.rem(me + i, n)
-        forward_copy(peer, me).wait_send()
-        back_copy(peer, me).wait_send()
-        return carry
-
-    lax.fori_loop(1, n, drain, 0)
-
-    @pl.when(me < n - 1)
-    def _():
-        target_copy(after, 0).wait_send()
-        strip_copy(after, 0).wait_send()
-
-    @pl.when(me > 0)
-    def _():
-        target_copy(before, 1).wait_send()
-        strip_copy(before, 1).wait_send()
-
     for copy in sent:
         copy.wait_send()
     for i in range(1, nv):
         camera_copy(lax.rem(mv + i, nv), mv).wait_send()
 
 
-def row_order_kernel(wide_hbm, rad_hbm, grad_ref, radiance_ref, wide_ref, sems):
+def row_order_kernel(wide_hbm, rad_hbm, grad_hbm, radiance_hbm, grad_ref, wide_ref, sems, out_sems):
     groups = [(first, min(8, FEAT - first)) for first in range(0, FEAT, 8)]
-    loads = [pltpu.make_async_copy(rad_hbm, radiance_ref, sems.at[len(groups)])]
+    loads = [pltpu.make_async_copy(rad_hbm, radiance_hbm, sems.at[len(groups)])]
+    stores = []
     for g, (first, size) in enumerate(groups):
         rows = pl.ds(first * HIGH, size * HIGH)
         loads.append(pltpu.make_async_copy(wide_hbm.at[rows], wide_ref.at[rows], sems.at[g]))
@@ -1057,7 +1106,11 @@
             grad_ref[first : first + size, h * COLS : (h + 1) * COLS] = wide_ref[
                 pl.ds(first * HIGH + h, size, stride=HIGH), :
             ]
-    loads[0].wait()
+        rows = pl.ds(first, size)
+        stores.append(pltpu.make_async_copy(grad_ref.at[rows], grad_hbm.at[rows], out_sems.at[g]))
+        stores[-1].start()
+    for copy in stores + loads[:1]:
+        copy.wait()
 
 
 def shards(n, nv, gaussians, send_index, tile_list, tile_length, camera, exposure, target):
@@ -1102,6 +1155,10 @@
         scratch((MAPS * 16, COLS)),
         scratch((MAPS * 16, COLS)),
         scratch((MAPS * 16, COLS)),
+        scratch((ROWS * 16, COLS)),
+        scratch((ROWS * 16, COLS)),
+        scratch((ROWS * 16, COLS)),
+        scratch((3 * MAPS * 16, 4 * COLS), BF16),
         scratch((3 * ROWS, COLS)),
         scratch((3 * TILES, LIST)),
         scratch((2 * SPLAT * halves, COLS)),
@@ -1142,8 +1199,13 @@
             jax.ShapeDtypeStruct((1, 3, ROWS, COLS), F32),
         ),
         in_specs=[pl.BlockSpec(memory_space=pl.ANY)] * 2,
-        out_specs=(vmem, vmem),
-        scratch_shapes=[scratch((FEAT * HIGH, COLS)), pltpu.SemaphoreType.DMA((9,))],
+        out_specs=(pl.BlockSpec(memory_space=pl.ANY),) * 2,
+        scratch_shapes=[
+            scratch((FEAT, HIGH * COLS)),
+            scratch((FEAT * HIGH, COLS)),
+            pltpu.SemaphoreType.DMA((9,)),
+            pltpu.SemaphoreType.DMA((8,)),
+        ],
         name="row_order",
     )(wide_grad, strip)
 

time: 62.6 us -> 59.8 us (0.955)
  Pallas kernels: 61.7 us -> 58.8 us
    pallas_call x1, Pallas kernels: 59.2 us -> 56.5 us  [shards(): pl.pallas_call(functools.partial(step_kernel, n, nv), out_shape=(jax.Shap...]
where the time goes in v2:
time: 59.8 us; the launch traced here: 59.5 us
  Pallas kernels  58.8 us (98%)
  between operations  0.64 us (1%)
    pallas_call x1, Pallas kernels, shards(): pl.pallas_call(functools.partial(step_kernel, n, nv), out_shape=(jax.Shap...  56.5 us
    pallas_call x1, Pallas kernels, shards(): pl.pallas_call(row_order_kernel, out_shape=(jax.ShapeDtypeStruct((FEAT, H...  2.33 us

profile of v2, /device:TPU:1, one launch (start us, length us, event | category | flops | bytes accessed | tf_op | source)
XLA Modules:
  0.0 59.5 jit_solution(8584126283495901387)
XLA Ops:
  0.6 56.5 %splat_step.1 = (f32[1888,128]{1,0:T(8,128)}, f32[1,3,16,128]{3,2,1,0:T(8,128)}) custom-call(f32[59,4096]{1,0:T(8,128)} %gauss_hbm.1, s32[1,64,128]{2,1,0:T(8,128)} %send_hbm.1, s32[1,8,256]{2,1,0:T(8,128)} %list_hbm.1, s32[1,8]{1,0:T(1,128)} %len_hbm.1, f32[1,5]{1,0:T(1,128)} %cam_hbm.1, f32[1,5]{1,0:T(1,128)} %expo_hbm.1, f32[1,15,16,128]{3,2,1,0:T(8,128)} %target_hbm.1), custom_call_target="tpu_custom_call" | custom-call | tf_op jit(solution)/shard_map/splat_step/pallas_call | solution.py:1181
  57.2 2.3 %row_order.1 = (f32[59,4096]{1,0:T(8,128)}, f32[1,3,16,128]{3,2,1,0:T(8,128)}) custom-call(f32[1888,128]{1,0:T(8,128)} %get-tuple-element.4.wide_hbm, f32[1,3,16,128]{3,2,1,0:T(8,128)} %get-tuple-element.5.rad_hbm), custom_call_target="tpu_custom_call" | custom-call | tf_op jit(solution)/shard_map/row_order/pallas_call | solution.py:1195

commit v3 on v2

--- a/solution.py
+++ b/solution.py
@@ -42,6 +42,7 @@
 TILES = 8
 LIST = 256
 ROWS = 16
+LOG2E = 1.4426950408889634
 COLS = 128
 CHANNELS = 15
 FIRST = 11
@@ -345,9 +346,6 @@
         [camera[i][0:1] for i in range(5)] + [jnp.zeros((3, COLS), F32)], axis=0
     )
 
-    for load in loads[2:]:
-        load.wait()
-    pl.semaphore_wait(barrier, n - 1 + nv - 1)
 
     def target_copy(peer, side):
         return pltpu.make_async_remote_copy(
@@ -427,6 +425,10 @@
         for i in range(group):
             peer = block * group + i
             out_ref[peer] = pick_ref[pl.ds(i, SPLAT, stride=group), :]
+        return carry
+
+    def send_group(step, carry):
+        block = lax.rem(my_group + shift_of(step), groups)
         for i in range(group):
             peer = block * group + lax.rem(me + i, group)
 
@@ -436,7 +438,17 @@
 
         return carry
 
-    lax.fori_loop(0, groups, gather_group, 0)
+    def gather_and_send(step, carry):
+        send_group(step, carry)
+        return gather_group(step + ahead, carry)
+
+    for load in loads[2:]:
+        load.wait()
+    ahead = min(2, groups)
+    lax.fori_loop(0, ahead, gather_group, 0)
+    pl.semaphore_wait(barrier, n - 1 + nv - 1)
+    lax.fori_loop(0, groups - ahead, gather_and_send, 0)
+    lax.fori_loop(groups - ahead, groups, send_group, 0)
     recv_ref[me] = out_ref[me]
     @pl.when(me < n - 1)
     def _():
@@ -528,12 +540,12 @@
         ox, oy, a, b, c = [splat_row(f, j) for f in range(5)]
         opacity = splat_row(SPLAT, j)
         dx = column_x - ox
-        square_part = (-0.5 * a) * dx * dx
-        cross_part = (-b) * dx
+        square_part = (-0.5 * LOG2E * a) * dx * dx
+        cross_part = (-LOG2E * b) * dx
         for y in range(16):
             dy = (y + 0.5 - 8.0) - oy
-            power = square_part + dy * cross_part + (-0.5 * c) * dy * dy
-            cover = opacity * jnp.exp(power)
+            power = square_part + dy * cross_part + (-0.5 * LOG2E * c) * dy * dy
+            cover = opacity * jnp.exp2(power)
             cover_ref[pixel_rows(j, y), :] = cover
             top, low = parts(jnp.log(1.0 - cover))
             pair_ref[y * 16 : y * 16 + 16, 0:LIST] = top

time: 59.8 us -> 58.9 us (0.985)
  Pallas kernels: 58.8 us -> 58.2 us
    pallas_call x1, Pallas kernels: 56.5 us -> 55.8 us  [shards(): pl.pallas_call(functools.partial(step_kernel, n, nv), out_shape=(jax.Shap...]
where the time goes in v3:
time: 58.9 us; the launch traced here: 58.8 us
  Pallas kernels  58.2 us (99%)
  between operations  0.64 us (1%)
    pallas_call x1, Pallas kernels, shards(): pl.pallas_call(functools.partial(step_kernel, n, nv), out_shape=(jax.Shap...  55.8 us
    pallas_call x1, Pallas kernels, shards(): pl.pallas_call(row_order_kernel, out_shape=(jax.ShapeDtypeStruct((FEAT, H...  2.33 us

profile of v3, /device:TPU:1, one launch (start us, length us, event | category | flops | bytes accessed | tf_op | source)
XLA Modules:
  0.0 58.8 jit_solution(7946732940551988306)
XLA Ops:
  0.6 55.8 %splat_step.1 = (f32[1888,128]{1,0:T(8,128)}, f32[1,3,16,128]{3,2,1,0:T(8,128)}) custom-call(f32[59,4096]{1,0:T(8,128)} %gauss_hbm.1, s32[1,64,128]{2,1,0:T(8,128)} %send_hbm.1, s32[1,8,256]{2,1,0:T(8,128)} %list_hbm.1, s32[1,8]{1,0:T(1,128)} %len_hbm.1, f32[1,5]{1,0:T(1,128)} %cam_hbm.1, f32[1,5]{1,0:T(1,128)} %expo_hbm.1, f32[1,15,16,128]{3,2,1,0:T(8,128)} %target_hbm.1), custom_call_target="tpu_custom_call" | custom-call | tf_op jit(solution)/shard_map/splat_step/pallas_call | solution.py:1193
  56.5 2.3 %row_order.1 = (f32[59,4096]{1,0:T(8,128)}, f32[1,3,16,128]{3,2,1,0:T(8,128)}) custom-call(f32[1888,128]{1,0:T(8,128)} %get-tuple-element.4.wide_hbm, f32[1,3,16,128]{3,2,1,0:T(8,128)} %get-tuple-element.5.rad_hbm), custom_call_target="tpu_custom_call" | custom-call | tf_op jit(solution)/shard_map/row_order/pallas_call | solution.py:1207

commit v4 on v3

--- a/solution.py
+++ b/solution.py
@@ -444,7 +444,7 @@
 
     for load in loads[2:]:
         load.wait()
-    ahead = min(2, groups)
+    ahead = min(3, groups)
     lax.fori_loop(0, ahead, gather_group, 0)
     pl.semaphore_wait(barrier, n - 1 + nv - 1)
     lax.fori_loop(0, groups - ahead, gather_and_send, 0)

time: 58.9 us -> 59.3 us (level)
  no operation moved by 1% of the time
where the time goes in v4:
time: 59.3 us; the launch traced here: 59.2 us
  Pallas kernels  58.6 us (99%)
  between operations  0.64 us (1%)
    pallas_call x1, Pallas kernels, shards(): pl.pallas_call(functools.partial(step_kernel, n, nv), out_shape=(jax.Shap...  56.2 us
    pallas_call x1, Pallas kernels, shards(): pl.pallas_call(row_order_kernel, out_shape=(jax.ShapeDtypeStruct((FEAT, H...  2.33 us

profile of v4, /device:TPU:1, one launch (start us, length us, event | category | flops | bytes accessed | tf_op | source)
XLA Modules:
  0.0 59.2 jit_solution(16500403730222788414)
XLA Ops:
  0.6 56.2 %splat_step.1 = (f32[1888,128]{1,0:T(8,128)}, f32[1,3,16,128]{3,2,1,0:T(8,128)}) custom-call(f32[59,4096]{1,0:T(8,128)} %gauss_hbm.1, s32[1,64,128]{2,1,0:T(8,128)} %send_hbm.1, s32[1,8,256]{2,1,0:T(8,128)} %list_hbm.1, s32[1,8]{1,0:T(1,128)} %len_hbm.1, f32[1,5]{1,0:T(1,128)} %cam_hbm.1, f32[1,5]{1,0:T(1,128)} %expo_hbm.1, f32[1,15,16,128]{3,2,1,0:T(8,128)} %target_hbm.1), custom_call_target="tpu_custom_call" | custom-call | tf_op jit(solution)/shard_map/splat_step/pallas_call | solution.py:1193
  56.9 2.3 %row_order.1 = (f32[59,4096]{1,0:T(8,128)}, f32[1,3,16,128]{3,2,1,0:T(8,128)}) custom-call(f32[1888,128]{1,0:T(8,128)} %get-tuple-element.4.wide_hbm, f32[1,3,16,128]{3,2,1,0:T(8,128)} %get-tuple-element.5.rad_hbm), custom_call_target="tpu_custom_call" | custom-call | tf_op jit(solution)/shard_map/row_order/pallas_call | solution.py:1207
